TPU v7x, 1024 devices: a whole 4x8x16 slice. The times are simulated.
1024 devices in a mesh: section: 4 (over x), expert: 32 (over z, y_lo), dp: 8 (over y_hi, core).
Axes of the slice: x: 4, y: 8 (y_hi: 4, y_lo: 2; y = y_hi * 2 + y_lo), z: 16, core: 2. Of those that a mesh axis runs over, the one named last changes fastest.
Arguments:
- routes: int32 [4, 4096, 8], P('section', 'expert'), may hold values from 0 to 63, all different within a row; in each aligned block of 128 rows (0 to 127, 128 to 255, ..., all dimensions but the last counted through in order) at most 24 rows name the same one
- weights: float32 [4, 4096, 8], P('section', 'expert'), may hold values from 0.02 to 0.25
- cotangent: bfloat16 [4, 4096, 7168], P('section', 'expert', 'dp'), may hold values from -6 to 6
- hidden: bfloat16 [4, 64, 768, 1024], P('section', 'expert'), may hold values from -6 to 6
Outputs:
- grad: bfloat16 [2, 64, 1024, 7168], P(None, 'expert', None, ('dp', 'section'))
Inputs may be any that keep to these rules, and one draw needn't show every extreme that they name: `routes`: in each aligned block of 128 token rows of a section, no expert is named more than 24 times, a bound that some block reaches.
All inputs are finite; a program needn't handle non-finite values.
Results may differ from a plain program's by a relative error of at most 0.0058.
Values may be sent and summed in bfloat16 or wider, within the bound.
A program may use at most 32 MiB of HBM per device.

v0:
```python
import math

import jax
import jax.numpy as jnp
from jax import lax
from jax.sharding import PartitionSpec as P


def local(routes, weights, cotangent, hidden):
    tok_rows = routes.shape[1]
    top_count = routes.shape[2]
    expert_dev = hidden.shape[1]
    slot_count = hidden.shape[2]
    hidden_units = hidden.shape[3]
    expert_count = lax.axis_size("expert")
    all_experts = expert_dev * expert_count
    capacity = slot_count // expert_count
    columns = cotangent.shape[2]
    section_count = lax.axis_size("section")
    width = columns // section_count
    flat_routes = routes.reshape(-1)
    onehot = (flat_routes[:, None] == jnp.arange(all_experts, dtype=jnp.int32)[None, :]).astype(
        jnp.int32
    )
    earlier = jnp.cumsum(onehot, axis=0) - onehot
    ranks = jnp.sum(earlier * onehot, axis=1)
    scaled = weights.reshape(tok_rows, top_count, 1) * cotangent.reshape(
        tok_rows, 1, columns
    ).astype(jnp.float32)
    scaled = scaled.astype(jnp.bfloat16).reshape(tok_rows * top_count, columns)
    outgoing = (
        jnp.zeros((all_experts, capacity, columns), jnp.bfloat16).at[flat_routes, ranks].set(scaled)
    )
    outgoing = outgoing.reshape(expert_count, expert_dev, capacity, columns)
    received = lax.all_to_all(outgoing, "expert", split_axis=0, concat_axis=0, tiled=True)
    saved = hidden.reshape(expert_dev, expert_count, capacity, hidden_units)
    routed = received.reshape(expert_count, expert_dev, capacity, section_count, width)
    partial_grad = jnp.einsum(
        "escf,secnw->enfw", saved, routed, preferred_element_type=jnp.float32
    ).astype(jnp.bfloat16)
    half_count = section_count // 2
    gathered = lax.all_to_all(partial_grad, "section", split_axis=1, concat_axis=0, tiled=True)
    ordered = gathered.reshape(section_count, expert_dev, hidden_units, width)
    paired = ordered[:half_count].astype(jnp.float32) + jnp.flip(ordered, axis=0)[
        :half_count
    ].astype(jnp.float32)
    factor = 2.0 / math.sqrt(slot_count)
    return (paired * factor).astype(jnp.bfloat16)


def solution(mesh):
    return jax.shard_map(
        local,
        mesh=mesh,
        in_specs=(
            P("section", "expert", None),
            P("section", "expert", None),
            P("section", "expert", "dp"),
            P("section", "expert", None, None),
        ),
        out_specs=P(None, "expert", None, ("dp", "section")),
        check_vma=False,
    )
```

profile of v0, /device:TPU:56, one launch (start us, length us, event | category | flops | bytes accessed | tf_op | source)
XLA Modules:
  0.0 258.2 jit_solution(4708808399679707389)
XLA Ops:
  0.0 0.0 copy-start
  0.0 0.9 copy.16
  0.9 0.1 eq.29
  1.0 0.1 eq.25
  1.1 0.1 reshape.92
  1.2 0.8 copy.21
  2.0 0.1 mul.28
  2.1 0.7 fusion.16
  2.8 31.1 %reduce-window.6 = s32[64,8,128]{2,1,0:T(8,128)S(1)} reduce-window(s32[64,8,128]{2,1,0:T(8,128)} %fusion.16, s32[]{:T(128)} %constant.6.clone.1), window={size=1x1x128 pad=0_0x0_0x127_0}, to_apply=%region_0.0 | reduce-window | flops 8323072 | bytes 524292 | tf_op jit(solution)/shard_map/reduce-window
  33.9 0.8 slice.25
  34.8 1.1 copy.19
  35.9 0.1 copy.20
  36.0 0.1 broadcast_add_fusion
  36.1 0.1 fusion.15
  36.2 0.8 and_reduce_fusion
  37.0 0.7 multiply_reduce_fusion
  37.7 1.7 bitcast_convert_fusion.1
  39.4 7.9 %scatter_custom_fusion = bf16[1536,896]{1,0:T(8,128)(2,1)} fusion(s32[1024]{0:T(1024)S(1)} %broadcast_select_fusion, f32[128,896]{1,0:T(8,128)} %bitcast_convert_fusion.1, f32[1024]{0:T(1024)S(1)} %mul.28, bf16[]{:T(256)} %constant.5.clone.1), kind=kCustom, calls=%fused_computation.10 | custom fusion | flops 1835008 | bytes 3215362
  47.3 148.6 %all_to_all.20 = bf16[32,2,24,896]{3,2,1,0:T(8,128)(2,1)} all-to-all(bf16[32,2,24,896]{3,2,1,0:T(8,128)(2,1)} %bitcast.57), channel_id=1, replica_groups=mesh['section'=4,'expert'=32,'dp'=8] {'expert'}, dimensions={0} | all-to-all | bytes 5505024 | tf_op jit(solution)/shard_map/all_to_all | solution.py:35
  195.9 8.1 %reshape.95 = bf16[32,2,24,4,224]{4,3,2,1,0:T(4,128)(2,1)} reshape(bf16[32,2,24,896]{3,2,1,0:T(8,128)(2,1)} %all_to_all.20) | data formatting | bytes 5505024 | tf_op jit(solution)/shard_map/reshape | solution.py:37
  204.0 0.0 copy-done
  204.0 5.3 %fusion = bf16[2,4,1024,224]{2,3,1,0:T(8,128)(2,1)S(1)} fusion(bf16[2,32,24,1024,1]{3,2,1,4,0:T(8,128)(2,1)S(1)} %bitcast.54, bf16[32,2,24,4,224]{4,3,2,1,0:T(4,128)(2,1)} %reshape.95), kind=kOutput, calls=%fused_computation.2 | convolution fusion | flops 2820407296 | bytes 9568256 | tf_op jit(solution)/shard_map/escf,secnw->enfw/dot_general | solution.py:38
  209.3 0.4 copy.23
  209.6 46.3 %all_to_all.21 = bf16[2,4,1024,224]{2,3,0,1:T(8,128)(2,1)S(1)} all-to-all(bf16[2,4,1024,224]{2,3,0,1:T(8,128)(2,1)S(1)} %copy.23), channel_id=1, replica_groups=mesh['section'=4,'expert'=32,'dp'=8] {'section'}, dimensions={1} | all-to-all | bytes 7340032 | tf_op jit(solution)/shard_map/all_to_all | solution.py:42
  256.0 0.1 slice_bitcast_fusion
  256.1 2.1 fusion.2
  (4 shorter events, 0.0 us)
Async XLA Ops:
  0.0 204.0 %copy-start = (bf16[1,2,768,1024]{3,2,1,0:T(8,128)(2,1)S(1)}, bf16[1,2,768,1024]{3,2,1,0:T(8,128)(2,1)}, u32[]{:S(2)}) copy-start(bf16[1,2,768,1024]{3,2,1,0:T(8,128)(2,1)} %param.7) | copy-start | bytes 9437188
where the time goes:
time: 260 us; the launch traced here: 258 us
  blocking collectives  195 us (75%)
  other arithmetic  45.3 us (17%)
  local copies, waits for them, and re-layouts  12.7 us (5%)
  matrix products  5.25 us (2%)
    all_to_all x1, blocking collectives, local(): lax.all_to_all(outgoing, 'expert', split_axis=0, concat_axis=0, tiled=True)  149 us
    all_to_all x1, blocking collectives, local(): lax.all_to_all(partial_grad, 'section', split_axis=1, concat_axis=0, tile...  46.3 us
    another operation x3, other arithmetic  31.3 us
    unnamed x4, other arithmetic  9.35 us
    reshape x1, local copies, waits for them, and re-layouts, local(): received.reshape(expert_count, expert_dev, capacity, section_count, width)  8.07 us
    dot_general x1, matrix products, local(): jnp.einsum('escf,secnw->enfw', saved, routed, preferred_element_type=jnp....  5.25 us

commit v1 on v0

v1 whole, which is shorter than its diff:
```python
import functools
import math

import jax
import jax.numpy as jnp
from jax import lax
from jax.experimental import pallas as pl
from jax.experimental.pallas import tpu as pltpu
from jax.sharding import PartitionSpec as P

MESH = pl.DeviceIdType.MESH
BF = jnp.bfloat16
F32 = jnp.float32
LANE = 128
DEPTH = 3


def kernel(
    cfg,
    routes_ref,
    weights_ref,
    cot_ref,
    hid_ref,
    out_ref,
    cot_t,
    buf_a,
    buf_b,
    mir_a,
    hid_own,
    hid_mir,
    hid_t,
    upper,
    sel,
    scale,
    mine,
    other,
    routed,
    out_a,
    out_b,
    ring_s,
    ring_r,
    mir_s,
    mir_r,
    hid_l,
    hid_s,
    hid_r,
    sib_s,
    sib_r,
    pair_s,
    pair_r,
    lat_s,
    lat_r,
    out_l,
):
    half, cap, width, pieces, tops = cfg
    blocks = 2 * half
    rows = 2 * cap
    s = lax.axis_index("section")
    e = lax.axis_index("expert")
    d = lax.axis_index("dp")
    z = e // 2
    yl = lax.rem(e, 2)
    core = lax.rem(d, 2)
    n_exp = 2 * blocks
    up = {"expert": lax.rem(e + 2, n_exp)}
    down = {"expert": lax.rem(e + n_exp - 2, n_exp)}
    partner = {"expert": e + 1 - 2 * yl}
    sibling = {"dp": d + 1 - 2 * core}
    mirror_s = 3 - s
    mirror = {"section": mirror_s}
    lat_sec = s + 1 - 2 * lax.rem(s, 2)
    lateral = {"section": lat_sec}
    pair_index = jnp.where(s < 2, s, 3 - s)
    factor = 2.0 / math.sqrt(rows * blocks)
    bufs = (buf_a, buf_b)

    def remote(src, dst, ss, rs, where):
        return pltpu.make_async_remote_copy(
            src_ref=src, dst_ref=dst, send_sem=ss, recv_sem=rs, device_id=where, device_id_type=MESH
        )

    def ring(ch, way, sec, k):
        if way == 0:
            dst, src = 2 * k - 1, jnp.maximum(2 * k - 3, 0)
        else:
            dst, src = jnp.minimum(2 * k, blocks - 1), 2 * k - 2
        buf = bufs[ch]
        return remote(
            buf.at[sec, src],
            buf.at[sec, dst],
            ring_s.at[ch, way, sec, k],
            ring_r.at[ch, way, sec, k],
            up if way == 0 else down,
        )

    def hid_local(ex, f):
        return pltpu.make_async_copy(
            hid_ref.at[ex, :, pl.ds(pl.multiple_of(f * LANE, LANE), LANE)],
            hid_own.at[ex, f],
            hid_l.at[ex, f],
        )

    def hid_send(f):
        return remote(
            hid_ref.at[core, :, pl.ds(pl.multiple_of(f * LANE, LANE), LANE)],
            hid_mir.at[core, f],
            hid_s.at[f],
            hid_r.at[f],
            mirror,
        )

    def sib_send(f):
        return remote(hid_mir.at[core, f], hid_mir.at[core, f], sib_s.at[f], sib_r.at[f], sibling)

    def pair_copy(ch, k, first, count):
        return remote(
            other.at[ch, pl.ds(first, count)],
            mine.at[ch, yl, pl.ds(first, count)],
            pair_s.at[ch, k],
            pair_r.at[ch, k],
            partner,
        )

    def lat_send(f):
        return remote(
            out_a.at[f],
            out_ref.at[pair_index, :, pl.ds(pl.multiple_of(f * LANE, LANE), LANE), :],
            lat_s.at[f],
            lat_r.at[f],
            lateral,
        )

    barrier = pltpu.get_barrier_semaphore()
    for where in (up, down, partner, sibling, mirror, lateral):
        pl.semaphore_signal(barrier, inc=1, device_id=where, device_id_type=MESH)
    for ex in range(2):
        for f in range(pieces):
            hid_local(ex, f).start()
    cot_t[...] = cot_ref[...].T
    routes = routes_ref[...].astype(F32)
    w0 = weights_ref[...]
    w1 = w0.astype(BF)
    rest = w0 - w1.astype(F32)
    w2 = rest.astype(BF)
    w3 = (rest - w2.astype(F32)).astype(BF)
    info = jnp.concatenate(
        [routes, w1.astype(F32), w2.astype(F32), w3.astype(F32)], axis=0
    ).astype(BF)

    def columns(section):
        return cot_t[pl.ds(pl.multiple_of(section * width, 16), width), :]

    buf_a[0, 0, 0:width, :] = columns(lat_sec)
    buf_a[0, 0, width : width + 4 * tops, :] = info
    buf_b[0, 0] = columns(s)
    mir_a[0, 0:width, :] = columns(mirror_s + 1 - 2 * lax.rem(mirror_s, 2))
    mir_a[0, width : width + 4 * tops, :] = info
    mir_a[1, 0:width, :] = columns(mirror_s)
    row = lax.broadcasted_iota(jnp.int32, (LANE, LANE), 0)
    col = lax.broadcasted_iota(jnp.int32, (LANE, LANE), 1)
    upper[...] = jnp.where(row < col, 1.0, 0.0).astype(BF)
    pl.semaphore_wait(barrier, 6)

    mir_copies = (
        remote(mir_a.at[0], buf_a.at[1, 0], mir_s.at[0], mir_r.at[0], mirror),
        remote(mir_a.at[1, pl.ds(0, width)], buf_b.at[1, 0], mir_s.at[1], mir_r.at[1], mirror),
    )
    for copy in mir_copies:
        copy.start()
    for way in range(2):
        ring(0, way, 0, 1).start()
    for f in range(min(DEPTH, pieces)):
        hid_send(f).start()

    experts = [4 * z + 2 * yl, 4 * z + 2 * yl + 1, 4 * z + 2 - 2 * yl, 4 * z + 3 - 2 * yl]

    def build(slots):
        masks, gains, combos = [], [], [(sec, slot) for slot in slots for sec in range(2)]
        for sec, slot in combos:
            data = buf_a[sec, slot, width : width + 4 * tops, :].astype(F32)
            named = data[0:tops]
            gain = data[tops : 2 * tops] + data[2 * tops : 3 * tops] + data[3 * tops : 4 * tops]
            for ex in experts:
                hit = jnp.where(named == ex.astype(F32), 1.0, 0.0)
                masks.append(jnp.sum(hit, axis=0, keepdims=True))
                gains.append(jnp.sum(hit * gain, axis=0, keepdims=True))
        mask = jnp.concatenate(masks, axis=0)
        rank = jnp.dot(mask.astype(BF), upper[...], preferred_element_type=F32)
        rank = jnp.where(mask > 0.5, rank, -1.0)
        place = lax.broadcasted_iota(jnp.int32, (cap, LANE), 0).astype(F32)
        for i, (sec, slot) in enumerate(combos):
            hots, weights = [], []
            for j in range(4):
                n = 4 * i + j
                hot = place == rank[n : n + 1]
                hots.append(jnp.where(hot, 1.0, 0.0))
                one = jnp.sum(jnp.where(hot, gains[n], 0.0), axis=1, keepdims=True)
                weights.append(jnp.broadcast_to(one, (cap, LANE)))
            sel[sec, slot] = jnp.concatenate(hots, axis=0).astype(BF)
            scale[sec, slot] = jnp.concatenate(weights, axis=0)

    def pick(ch, slots):
        for slot in slots:
            for sec in range(2):
                hot = sel[sec, slot]
                data = bufs[ch][sec, slot, 0:width, :]
                got = lax.dot_general(
                    hot, data, (((1,), (1,)), ((), ())), preferred_element_type=F32
                )
                gain = scale[sec, slot]
                parts = -(-width // LANE)
                gain = jnp.concatenate([gain] * parts, axis=1)[:, :width]
                got = (got * gain).astype(BF)
                mine[ch, yl, slot, sec] = got[0:rows]
                other[ch, slot, sec] = got[rows : 2 * rows]

    def merge(ch, k, slots):
        pair_copy(ch, k, slots[0], len(slots)).wait()
        for slot in slots:
            for sec in range(2):
                first = mine[ch, 0, slot, sec].astype(F32)
                second = mine[ch, 1, slot, sec].astype(F32)
                at = pl.ds(pl.multiple_of(slot * rows, 16), rows)
                for ex in range(2):
                    part = slice(ex * cap, (ex + 1) * cap)
                    routed[ch, sec, ex, at, :] = jnp.concatenate(
                        [first[part], second[part]], axis=0
                    ).astype(BF)

    def turn(sec, ex, f, source):
        got = []
        for n in range(blocks):
            step = (n + 1) // 2
            sign = -1 if n % 2 == 1 else 1
            zz = lax.rem(z + sign * step + blocks, blocks)
            got.append(source[ex, f, pl.ds(pl.multiple_of(zz * rows, 16), rows), :])
        at = pl.ds(pl.multiple_of(f * LANE, LANE), LANE)
        hid_t[sec, ex, at, :] = jnp.concatenate(got, axis=0).T

    def turn_own(f):
        for ex in range(2):
            hid_local(ex, f).wait()
            turn(0, ex, f, hid_own)

    def product(ch, ex, at):
        total = None
        for sec in range(2):
            term = jnp.dot(hid_t[sec, ex, at, :], routed[ch, sec, ex], preferred_element_type=F32)
            total = term if total is None else total + term
        return (total * factor).astype(BF)

    def send_first(f):
        at = pl.ds(pl.multiple_of(f * LANE, LANE), LANE)
        for ex in range(2):
            out_a[f, ex] = product(0, ex, at)
        lat_send(f).start()

    def slots_of(k):
        return (2 * k - 1, 2 * k)

    def receive(ch, k, sends):
        for sec in range(2):
            for way in range(2):
                ring(ch, way, sec, k).wait_recv()
                if sends == 2 or (sends == 1 and way == sec):
                    ring(ch, way, sec, k + 1).start()

    def sent(ch, k):
        for sec in range(2):
            for way in range(2):
                ring(ch, way, sec, k).wait_send()

    def mirror_piece(f):
        copy = hid_send(f)
        copy.wait()
        sib_send(f).start()

    mir_copies[0].wait()
    for way in range(2):
        ring(0, way, 1, 1).start()
    build((0,))
    pick(0, (0,))
    pair_copy(0, 0, 0, 1).start()
    mir_copies[1].wait()

    def steps(ch, j, last):
        k = 2 * j + 1
        receive(ch, k, 1 if last else 2)
        if ch == 0:
            build(slots_of(k))
        pick(ch, slots_of(k))
        pair_copy(ch, k, slots_of(k)[0], 2).start()
        sent(ch, k)
        if last is True and half == 2:
            merge(ch, 0, (0,))
        elif last:
            merge(ch, k - 1, slots_of(k - 1))
        else:

            @pl.when(j == 0)
            def _():
                merge(ch, 0, (0,))

            @pl.when(j > 0)
            def _():
                merge(ch, k - 1, slots_of(k - 1))

        if ch == 0:
            turn_own(2 * j)
        else:
            send_first(2 * j)

        k = k + 1
        if last:
            for way in range(2):
                ring(ch, way, way, k).wait_recv()
            if ch == 0:
                for way in range(2):
                    for sec in range(2):
                        ring(1, way, sec, 1).start()
        else:
            receive(ch, k, 2)
        f = j if ch == 0 else pieces // 2 + j
        mirror_piece(f)
        if isinstance(f, int):
            if f + DEPTH < pieces:
                hid_send(f + DEPTH).start()
        elif ch == 0:

            @pl.when(f + DEPTH < pieces)
            def _():
                hid_send(f + DEPTH).start()
        else:

            @pl.when(f + DEPTH < pieces)
            def _():
                hid_send(f + DEPTH).start()

        at = (2 * half - 1,) if last else slots_of(k)
        if ch == 0:
            build(at)
        pick(ch, at)
        pair_copy(ch, k, at[0], len(at)).start()
        if last:
            for way in range(2):
                ring(ch, way, way, k).wait_send()
        else:
            sent(ch, k)
        merge(ch, k - 1, slots_of(k - 1))
        if ch == 0:
            turn_own(2 * j + 1)
        sib_send(f).wait()
        for ex in range(2):
            turn(1, ex, f, hid_mir)
        if ch == 1:
            send_first(2 * j + 1)

    def whole(ch):
        pairs = half // 2
        if pairs > 1:

            def body(j, carry):
                steps(ch, j, False)
                return carry

            lax.fori_loop(0, pairs - 1, body, 0)
        steps(ch, pairs - 1, True)

    whole(0)
    pick(1, (0,))
    pair_copy(1, 0, 0, 1).start()
    merge(0, half, (2 * half - 1,))

    whole(1)
    merge(1, half, (2 * half - 1,))

    def out_copy(f):
        at = pl.ds(pl.multiple_of(f * LANE, LANE), LANE)
        return pltpu.make_async_copy(
            out_b.at[f], out_ref.at[pair_index, :, at, :], out_l.at[f]
        )

    def finish(f, carry):
        at = pl.ds(pl.multiple_of(f * LANE, LANE), LANE)
        for ex in range(2):
            out_b[f, ex] = product(1, ex, at)
        out_copy(f).start()
        return carry

    lax.fori_loop(0, pieces, finish, 0)

    def close(f, carry):
        lat_send(f).wait()
        out_copy(f).wait()
        return carry

    lax.fori_loop(0, pieces, close, 0)


def local(routes, weights, cotangent, hidden):
    tokens = routes.shape[1]
    tops = routes.shape[2]
    slot_count, units = hidden.shape[2], hidden.shape[3]
    n_exp = lax.axis_size("expert")
    sections = lax.axis_size("section")
    cap = slot_count // n_exp
    rows = 2 * cap
    half = n_exp // 4
    blocks = 2 * half
    width = cotangent.shape[2] // sections
    pieces = units // LANE
    cfg = (half, cap, width, pieces, tops)
    vmem = pl.BlockSpec(memory_space=pltpu.VMEM)
    hbm = pl.BlockSpec(memory_space=pl.ANY)
    dma = pltpu.SemaphoreType.DMA
    return pl.pallas_call(
        functools.partial(kernel, cfg),
        out_shape=jax.ShapeDtypeStruct((2, 2, units, width), BF),
        in_specs=[vmem, vmem, vmem, hbm],
        out_specs=hbm,
        scratch_shapes=[
            pltpu.VMEM((sections * width, tokens), BF),
            pltpu.VMEM((2, blocks, width + 4 * tops, tokens), BF),
            pltpu.VMEM((2, blocks, width, tokens), BF),
            pltpu.VMEM((2, width + 4 * tops, tokens), BF),
            pltpu.VMEM((2, pieces, slot_count, LANE), BF),
            pltpu.VMEM((2, pieces, slot_count, LANE), BF),
            pltpu.VMEM((2, 2, units, slot_count), BF),
            pltpu.VMEM((tokens, tokens), BF),
            pltpu.VMEM((2, blocks, 2 * rows, tokens), BF),
            pltpu.VMEM((2, blocks, 2 * rows, tokens), F32),
            pltpu.VMEM((2, 2, blocks, 2, rows, width), BF),
            pltpu.VMEM((2, blocks, 2, rows, width), BF),
            pltpu.VMEM((2, 2, 2, slot_count, width), BF),
            pltpu.VMEM((pieces, 2, LANE, width), BF),
            pltpu.VMEM((pieces, 2, LANE, width), BF),
            dma((2, 2, 2, half + 1)),
            dma((2, 2, 2, half + 1)),
            dma((2,)),
            dma((2,)),
            dma((2, pieces)),
            dma((pieces,)),
            dma((pieces,)),
            dma((pieces,)),
            dma((pieces,)),
            dma((2, half + 1)),
            dma((2, half + 1)),
            dma((pieces,)),
            dma((pieces,)),
            dma((pieces,)),
        ],
        compiler_params=pltpu.CompilerParams(
            collective_id=0, has_side_effects=True, vmem_limit_bytes=52 * 1024 * 1024
        ),
        cost_estimate=pl.CostEstimate(
            flops=8 * units * slot_count * width * 4, bytes_accessed=8 << 20, transcendentals=0
        ),
    )(
        jnp.swapaxes(routes, 1, 2)[0],
        jnp.swapaxes(weights, 1, 2)[0],
        cotangent[0],
        hidden[0],
    )


def solution(mesh):
    return jax.shard_map(
        local,
        mesh=mesh,
        in_specs=(
            P("section", "expert", None),
            P("section", "expert", None),
            P("section", "expert", "dp"),
            P("section", "expert", None, None),
        ),
        out_specs=P(None, "expert", None, ("dp", "section")),
        check_vma=False,
    )
```

time: 260 us -> 98.3 us (0.38)
  blocking collectives: 195 us -> 0 us
  Pallas kernels: 0 us -> 91.5 us
  other arithmetic: 45.3 us -> 0 us
  local copies, waits for them, and re-layouts: 12.7 us -> 6.21 us
  matrix products: 5.25 us -> 0 us
    all_to_all x2 -> x0, blocking collectives: 195 us -> none  [the longest x1 149 us: local(): lax.all_to_all(outgoing, 'expert', split_axis=0, concat_axis=0, tiled=True)]
    pallas_call x0 -> x1, Pallas kernels: none -> 91.5 us  [local(): pl.pallas_call(functools.partial(kernel, cfg), out_shape=jax.ShapeDtypeSt...]
    another operation x3 -> x0, other arithmetic: 31.3 us -> none
    unnamed x4 -> x0, other arithmetic: 9.35 us -> none
    reshape x2 -> x0, local copies, waits for them, and re-layouts: 8.17 us -> none  [the longest x1 8.07 us: local(): received.reshape(expert_count, expert_dev, capacity, section_count, width)]
    dot_general x1 -> x0, matrix products: 5.25 us -> none  [local(): jnp.einsum('escf,secnw->enfw', saved, routed, preferred_element_type=jnp....]
    convert_element_type x3 -> x0, other arithmetic: 4.57 us -> none  [the longest x1 2.11 us: local(): return (paired * factor).astype(jnp.bfloat16)]
    pallas_call x0 -> x1, local copies, waits for them, and re-layouts: none -> 3.9 us  [local(): pl.pallas_call(functools.partial(kernel, cfg), out_shape=jax.ShapeDtypeSt...]
where the time goes in v1:
time: 98.3 us; the launch traced here: 97.8 us
  Pallas kernels  91.5 us (93%)
  local copies, waits for them, and re-layouts  6.21 us (6%)
    pallas_call x1, Pallas kernels, local(): pl.pallas_call(functools.partial(kernel, cfg), out_shape=jax.ShapeDtypeSt...  91.5 us
    pallas_call x1, local copies, waits for them, and re-layouts, local(): pl.pallas_call(functools.partial(kernel, cfg), out_shape=jax.ShapeDtypeSt...  3.9 us
    unnamed x6, local copies, waits for them, and re-layouts  2.31 us

profile of v1, /device:TPU:56, one launch (start us, length us, event | category | flops | bytes accessed | tf_op | source)
XLA Modules:
  0.0 97.8 jit_solution(18346460360038717440)
XLA Ops:
  0.0 0.0 copy-start
  0.0 0.9 copy-done
  0.9 0.0 copy-start.1
  0.9 0.7 copy-done.1
  1.6 0.0 copy-start.2
  1.6 0.7 copy-done.2
  2.3 91.5 %shard_map.46 = bf16[2,2,1024,224]{3,2,1,0:T(8,128)(2,1)} custom-call(s32[8,128]{1,0:T(8,128)S(1)} %bitcast.9, f32[8,128]{1,0:T(8,128)S(1)} %bitcast.10, bf16[128,896]{1,0:T(8,128)(2,1)S(1)} %bitcast.8, bf16[2,768,1024]{2,1,0:T(8,128)(2,1)} %bitcast.11), custom_call_target="tpu_custom_call" | custom-call | flops 5637144576 | bytes 8388608 | tf_op jit(solution)/shard_map/pallas_call | solution.py:416
  93.9 3.9 %copy.5 = bf16[2,2,1024,224]{2,3,1,0:T(8,128)(2,1)} copy(bf16[2,2,1024,224]{3,2,1,0:T(8,128)(2,1)} %shard_map.46) | data formatting | bytes 3670016 | tf_op jit(solution)/shard_map/pallas_call | solution.py:416
Async XLA Ops:
  0.0 0.9 copy-start
  0.9 0.7 copy-start.1
  1.6 0.7 copy-start.2

commit v2 on v1

--- a/solution.py
+++ b/solution.py
@@ -17,11 +17,15 @@
 
 def kernel(
     cfg,
+    routes_hbm,
+    weights_hbm,
+    cot_hbm,
+    hid_ref,
+    out_ref,
     routes_ref,
     weights_ref,
     cot_ref,
-    hid_ref,
-    out_ref,
+    arg_sem,
     cot_t,
     buf_a,
     buf_b,
@@ -37,6 +41,7 @@
     routed,
     out_a,
     out_b,
+    total,
     ring_s,
     ring_r,
     mir_s,
@@ -79,17 +84,19 @@
             src_ref=src, dst_ref=dst, send_sem=ss, recv_sem=rs, device_id=where, device_id_type=MESH
         )
 
-    def ring(ch, way, sec, k):
+    def ring(ch, way, sec, k, h):
         if way == 0:
             dst, src = 2 * k - 1, jnp.maximum(2 * k - 3, 0)
         else:
             dst, src = jnp.minimum(2 * k, blocks - 1), 2 * k - 2
         buf = bufs[ch]
+        count = (width + 4 * tops if ch == 0 else width) // 2
+        part = pl.ds(h * count, count)
         return remote(
-            buf.at[sec, src],
-            buf.at[sec, dst],
-            ring_s.at[ch, way, sec, k],
-            ring_r.at[ch, way, sec, k],
+            buf.at[sec, src, part],
+            buf.at[sec, dst, part],
+            ring_s.at[ch, way, sec, k, h],
+            ring_r.at[ch, way, sec, k, h],
             up if way == 0 else down,
         )
 
@@ -124,7 +131,7 @@
     def lat_send(f):
         return remote(
             out_a.at[f],
-            out_ref.at[pair_index, :, pl.ds(pl.multiple_of(f * LANE, LANE), LANE), :],
+            out_ref.at[pair_index, :, :, pl.ds(pl.multiple_of(f * LANE, LANE), LANE)],
             lat_s.at[f],
             lat_r.at[f],
             lateral,
@@ -133,6 +140,16 @@
     barrier = pltpu.get_barrier_semaphore()
     for where in (up, down, partner, sibling, mirror, lateral):
         pl.semaphore_signal(barrier, inc=1, device_id=where, device_id_type=MESH)
+    loads = [
+        pltpu.make_async_copy(src, dst, arg_sem.at[i])
+        for i, (src, dst) in enumerate(
+            ((cot_hbm, cot_ref), (routes_hbm, routes_ref), (weights_hbm, weights_ref))
+        )
+    ]
+    for load in loads:
+        load.start()
+    for load in loads:
+        load.wait()
     for ex in range(2):
         for f in range(pieces):
             hid_local(ex, f).start()
@@ -165,12 +182,10 @@
         remote(mir_a.at[0], buf_a.at[1, 0], mir_s.at[0], mir_r.at[0], mirror),
         remote(mir_a.at[1, pl.ds(0, width)], buf_b.at[1, 0], mir_s.at[1], mir_r.at[1], mirror),
     )
-    for copy in mir_copies:
-        copy.start()
-    for way in range(2):
-        ring(0, way, 0, 1).start()
-    for f in range(min(DEPTH, pieces)):
-        hid_send(f).start()
+    mir_copies[0].start()
+    for h in range(2):
+        for way in range(2):
+            ring(0, way, 0, 1, h).start()
 
     experts = [4 * z + 2 * yl, 4 * z + 2 * yl + 1, 4 * z + 2 - 2 * yl, 4 * z + 3 - 2 * yl]
 
@@ -242,17 +257,28 @@
             hid_local(ex, f).wait()
             turn(0, ex, f, hid_own)
 
-    def product(ch, ex, at):
-        total = None
+    def product(ch, ex, at, depth):
+        amount = None
         for sec in range(2):
-            term = jnp.dot(hid_t[sec, ex, at, :], routed[ch, sec, ex], preferred_element_type=F32)
-            total = term if total is None else total + term
-        return (total * factor).astype(BF)
+            term = jnp.dot(
+                hid_t[sec, ex, at, depth], routed[ch, sec, ex, depth, :], preferred_element_type=F32
+            )
+            amount = term if amount is None else amount + term
+        return amount
+
+    early_rows = (2 * half - 5) * rows // LANE * LANE
+    wide = 2 * LANE
+
+    def begin(f, carry):
+        at = pl.ds(pl.multiple_of(f * wide, wide), wide)
+        for ex in range(2):
+            total[ex, at, :] = product(1, ex, at, slice(0, early_rows))
+        return carry
 
     def send_first(f):
         at = pl.ds(pl.multiple_of(f * LANE, LANE), LANE)
         for ex in range(2):
-            out_a[f, ex] = product(0, ex, at)
+            out_a[f, ex] = (product(0, ex, at, slice(None)) * factor).astype(BF).T
         lat_send(f).start()
 
     def slots_of(k):
@@ -260,103 +286,126 @@
 
     def receive(ch, k, sends):
         for sec in range(2):
-            for way in range(2):
-                ring(ch, way, sec, k).wait_recv()
-                if sends == 2 or (sends == 1 and way == sec):
-                    ring(ch, way, sec, k + 1).start()
-
-    def sent(ch, k):
+            for h in range(2):
+                for way in range(2):
+                    if sends == 0 and way != sec:
+                        continue
+                    ring(ch, way, sec, k, h).wait_recv()
+                    if sends == 2 or (sends == 1 and way == sec):
+                        ring(ch, way, sec, k + 1, h).start()
+
+    def sent(ch, k, far=False):
         for sec in range(2):
-            for way in range(2):
-                ring(ch, way, sec, k).wait_send()
+            for h in range(2):
+                for way in range(2):
+                    if not far or way == sec:
+                        ring(ch, way, sec, k, h).wait_send()
+
+    def when(condition, action):
+        if isinstance(condition, bool):
+            if condition:
+                action()
+        else:
+            pl.when(condition)(action)
 
     def mirror_piece(f):
-        copy = hid_send(f)
-        copy.wait()
+        hid_send(f).wait()
         sib_send(f).start()
+        when(f + DEPTH < pieces, lambda: hid_send(f + DEPTH).start())
+
+    def turn_piece(f):
+        sib_send(f).wait()
+        for ex in range(2):
+            turn(1, ex, f, hid_mir)
 
     mir_copies[0].wait()
-    for way in range(2):
-        ring(0, way, 1, 1).start()
+    for h in range(2):
+        for way in range(2):
+            ring(0, way, 1, 1, h).start()
+    mir_copies[1].start()
+    for f in range(min(DEPTH, pieces)):
+        hid_send(f).start()
     build((0,))
     pick(0, (0,))
     pair_copy(0, 0, 0, 1).start()
-    mir_copies[1].wait()
+
+    pairs = half // 2
+    lead = pairs // 2
+
+    def early(j, h):
+        sec, k = j % 2 if isinstance(j, int) else lax.rem(j, 2), j // 2 + 1
+        if isinstance(j, int):
+            if k >= 2:
+                for way in range(2):
+                    ring(1, way, sec, k - 1, h).wait_recv()
+        else:
+
+            @pl.when(k >= 2)
+            def _():
+                for way in range(2):
+                    ring(1, way, sec, k - 1, h).wait_recv()
+
+        for way in range(2):
+            ring(1, way, sec, k, h).start()
 
     def steps(ch, j, last):
         k = 2 * j + 1
-        receive(ch, k, 1 if last else 2)
+        if ch == 0:
+            receive(ch, k, 1 if last else 2)
+            when(j == 1, lambda: mir_copies[1].wait())
+            early(j, 0)
+        elif isinstance(j, int):
+            if k >= lead:
+                receive(ch, k, 1 if last else 2)
+        else:
+            when(k >= lead, lambda: receive(ch, k, 1 if last else 2))
         if ch == 0:
             build(slots_of(k))
         pick(ch, slots_of(k))
         pair_copy(ch, k, slots_of(k)[0], 2).start()
-        sent(ch, k)
-        if last is True and half == 2:
-            merge(ch, 0, (0,))
-        elif last:
-            merge(ch, k - 1, slots_of(k - 1))
-        else:
-
-            @pl.when(j == 0)
-            def _():
-                merge(ch, 0, (0,))
-
-            @pl.when(j > 0)
-            def _():
-                merge(ch, k - 1, slots_of(k - 1))
-
+        when(k >= 3, lambda: merge(ch, k - 2, slots_of(k - 2)))
         if ch == 0:
+            when(j >= 2, lambda: turn_piece(j - 2))
             turn_own(2 * j)
         else:
-            send_first(2 * j)
+            piece = pairs - 1 + 2 * j
+            when(piece - 1 < pieces, lambda: turn_piece(piece - 1))
+            when(piece < pieces, lambda: mirror_piece(piece))
+
+            def rest_of_first():
+                merge(0, half - 1, slots_of(half - 1))
+                merge(0, half, (2 * half - 1,))
+
+            when(j == 0, rest_of_first)
+            more = (3 * j - 1 < pieces) if isinstance(j, int) else (j >= 1) & (3 * j - 1 < pieces)
+            if not isinstance(j, int) or j >= 1:
+                when(more, lambda: send_first(3 * j - 1))
+            if last:
+                lax.fori_loop(0, pieces // 2, begin, 0)
+        sent(ch, k)
 
         k = k + 1
-        if last:
-            for way in range(2):
-                ring(ch, way, way, k).wait_recv()
-            if ch == 0:
-                for way in range(2):
-                    for sec in range(2):
-                        ring(1, way, sec, 1).start()
-        else:
-            receive(ch, k, 2)
-        f = j if ch == 0 else pieces // 2 + j
-        mirror_piece(f)
-        if isinstance(f, int):
-            if f + DEPTH < pieces:
-                hid_send(f + DEPTH).start()
-        elif ch == 0:
-
-            @pl.when(f + DEPTH < pieces)
-            def _():
-                hid_send(f + DEPTH).start()
-        else:
-
-            @pl.when(f + DEPTH < pieces)
-            def _():
-                hid_send(f + DEPTH).start()
-
+        receive(ch, k, 0 if last else 2)
+        if ch == 0:
+            early(j, 1)
         at = (2 * half - 1,) if last else slots_of(k)
         if ch == 0:
             build(at)
         pick(ch, at)
         pair_copy(ch, k, at[0], len(at)).start()
-        if last:
-            for way in range(2):
-                ring(ch, way, way, k).wait_send()
+        when(j == 0, lambda: merge(ch, 0, (0,)))
+        when(j >= 1, lambda: merge(ch, k - 2, slots_of(k - 2)))
+        if ch == 0:
+            when(j >= 1, lambda: mirror_piece(j - 1))
+            turn_own(2 * j + 1)
         else:
-            sent(ch, k)
-        merge(ch, k - 1, slots_of(k - 1))
-        if ch == 0:
-            turn_own(2 * j + 1)
-        sib_send(f).wait()
-        for ex in range(2):
-            turn(1, ex, f, hid_mir)
-        if ch == 1:
-            send_first(2 * j + 1)
+            when(piece < pieces, lambda: turn_piece(piece))
+            when(piece + 1 < pieces, lambda: mirror_piece(piece + 1))
+            when(3 * j < pieces, lambda: send_first(3 * j))
+            when(3 * j + 1 < pieces, lambda: send_first(3 * j + 1))
+        sent(ch, k, far=last)
 
     def whole(ch):
-        pairs = half // 2
         if pairs > 1:
 
             def body(j, carry):
@@ -369,32 +418,38 @@
     whole(0)
     pick(1, (0,))
     pair_copy(1, 0, 0, 1).start()
-    merge(0, half, (2 * half - 1,))
 
     whole(1)
+    merge(1, half - 1, slots_of(half - 1))
     merge(1, half, (2 * half - 1,))
 
     def out_copy(f):
-        at = pl.ds(pl.multiple_of(f * LANE, LANE), LANE)
+        at = pl.ds(pl.multiple_of(f * wide, wide), wide)
         return pltpu.make_async_copy(
-            out_b.at[f], out_ref.at[pair_index, :, at, :], out_l.at[f]
+            out_b.at[f], out_ref.at[pair_index, :, :, at], out_l.at[f]
         )
 
     def finish(f, carry):
-        at = pl.ds(pl.multiple_of(f * LANE, LANE), LANE)
+        at = pl.ds(pl.multiple_of(f * wide, wide), wide)
         for ex in range(2):
-            out_b[f, ex] = product(1, ex, at)
+            late = total[ex, at, :] + product(1, ex, at, slice(early_rows, blocks * rows))
+            out_b[f, ex] = (late * factor).astype(BF).T
         out_copy(f).start()
         return carry
 
-    lax.fori_loop(0, pieces, finish, 0)
+    lax.fori_loop(0, pieces // 2, finish, 0)
 
     def close(f, carry):
         lat_send(f).wait()
+        return carry
+
+    lax.fori_loop(0, pieces, close, 0)
+
+    def close_own(f, carry):
         out_copy(f).wait()
         return carry
 
-    lax.fori_loop(0, pieces, close, 0)
+    lax.fori_loop(0, pieces // 2, close_own, 0)
 
 
 def local(routes, weights, cotangent, hidden):
@@ -410,15 +465,18 @@
     width = cotangent.shape[2] // sections
     pieces = units // LANE
     cfg = (half, cap, width, pieces, tops)
-    vmem = pl.BlockSpec(memory_space=pltpu.VMEM)
     hbm = pl.BlockSpec(memory_space=pl.ANY)
     dma = pltpu.SemaphoreType.DMA
-    return pl.pallas_call(
+    grad = pl.pallas_call(
         functools.partial(kernel, cfg),
-        out_shape=jax.ShapeDtypeStruct((2, 2, units, width), BF),
-        in_specs=[vmem, vmem, vmem, hbm],
+        out_shape=jax.ShapeDtypeStruct((2, 2, width, units), BF),
+        in_specs=[hbm, hbm, hbm, hbm],
         out_specs=hbm,
         scratch_shapes=[
+            pltpu.VMEM((tops, tokens), jnp.int32),
+            pltpu.VMEM((tops, tokens), F32),
+            pltpu.VMEM((tokens, sections * width), BF),
+            dma((3,)),
             pltpu.VMEM((sections * width, tokens), BF),
             pltpu.VMEM((2, blocks, width + 4 * tops, tokens), BF),
             pltpu.VMEM((2, blocks, width, tokens), BF),
@@ -432,10 +490,11 @@
             pltpu.VMEM((2, 2, blocks, 2, rows, width), BF),
             pltpu.VMEM((2, blocks, 2, rows, width), BF),
             pltpu.VMEM((2, 2, 2, slot_count, width), BF),
-            pltpu.VMEM((pieces, 2, LANE, width), BF),
-            pltpu.VMEM((pieces, 2, LANE, width), BF),
-            dma((2, 2, 2, half + 1)),
-            dma((2, 2, 2, half + 1)),
+            pltpu.VMEM((pieces, 2, width, LANE), BF),
+            pltpu.VMEM((pieces // 2, 2, width, 2 * LANE), BF),
+            pltpu.VMEM((2, units, width), F32),
+            dma((2, 2, 2, half + 1, 2)),
+            dma((2, 2, 2, half + 1, 2)),
             dma((2,)),
             dma((2,)),
             dma((2, pieces)),
@@ -447,10 +506,10 @@
             dma((2, half + 1)),
             dma((pieces,)),
             dma((pieces,)),
-            dma((pieces,)),
+            dma((pieces // 2,)),
         ],
         compiler_params=pltpu.CompilerParams(
-            collective_id=0, has_side_effects=True, vmem_limit_bytes=52 * 1024 * 1024
+            collective_id=0, has_side_effects=True, vmem_limit_bytes=63 * 1024 * 1024
         ),
         cost_estimate=pl.CostEstimate(
             flops=8 * units * slot_count * width * 4, bytes_accessed=8 << 20, transcendentals=0
@@ -461,6 +520,7 @@
         cotangent[0],
         hidden[0],
     )
+    return jnp.swapaxes(grad, 2, 3)
 
 
 def solution(mesh):

time: 98.3 us -> 87.5 us (0.89)
  Pallas kernels: 91.5 us -> 84.2 us
  local copies, waits for them, and re-layouts: 6.21 us -> 2.87 us
    pallas_call x1, Pallas kernels: 91.5 us -> 84.2 us  [local(): pl.pallas_call(functools.partial(kernel, cfg), out_shape=jax.ShapeDtypeSt...]
    pallas_call x1 -> x0, local copies, waits for them, and re-layouts: 3.9 us -> none  [local(): pl.pallas_call(functools.partial(kernel, cfg), out_shape=jax.ShapeDtypeSt...]
    unnamed x6 -> x1, local copies, waits for them, and re-layouts: 2.31 us -> 2.87 us
where the time goes in v2:
time: 87.5 us; the launch traced here: 87.1 us
  Pallas kernels  84.2 us (96%)
  local copies, waits for them, and re-layouts  2.87 us (3%)
    pallas_call x1, Pallas kernels, local(): pl.pallas_call(functools.partial(kernel, cfg), out_shape=jax.ShapeDtypeSt...  84.2 us
    unnamed x1, local copies, waits for them, and re-layouts  2.87 us

profile of v2, /device:TPU:56, one launch (start us, length us, event | category | flops | bytes accessed | tf_op | source)
XLA Modules:
  0.0 87.1 jit_solution(17201733398713095583)
XLA Ops:
  0.0 84.2 %shard_map.46 = bf16[2,2,224,1024]{3,2,1,0:T(8,128)(2,1)} custom-call(s32[8,128]{1,0:T(8,128)} %bitcast.12, f32[8,128]{1,0:T(8,128)} %bitcast.13, bf16[128,896]{1,0:T(8,128)(2,1)} %bitcast.11, bf16[2,768,1024]{2,1,0:T(8,128)(2,1)} %bitcast.10), custom_call_target="tpu_custom_call" | custom-call | flops 5637144576 | bytes 8388608 | tf_op jit(solution)/shard_map/pallas_call | solution.py:470
  84.2 2.9 %copy.6 = bf16[2,2,1024,224]{2,3,1,0:T(8,128)(2,1)} copy(bf16[2,2,1024,224]{2,3,1,0:T(8,128)(2,1)} %bitcast.9) | data formatting | bytes 3670016

commit v3 on v2

--- a/solution.py
+++ b/solution.py
@@ -84,14 +84,18 @@
             src_ref=src, dst_ref=dst, send_sem=ss, recv_sem=rs, device_id=where, device_id_type=MESH
         )
 
+    def half_of(ch, h):
+        total_rows = width + 2 * tops if ch == 0 else width
+        first = (total_rows // 2 + 15) // 16 * 16
+        return pl.ds(0, first) if h == 0 else pl.ds(first, total_rows - first)
+
     def ring(ch, way, sec, k, h):
         if way == 0:
             dst, src = 2 * k - 1, jnp.maximum(2 * k - 3, 0)
         else:
             dst, src = jnp.minimum(2 * k, blocks - 1), 2 * k - 2
         buf = bufs[ch]
-        count = (width + 4 * tops if ch == 0 else width) // 2
-        part = pl.ds(h * count, count)
+        part = half_of(ch, h)
         return remote(
             buf.at[sec, src, part],
             buf.at[sec, dst, part],
@@ -150,51 +154,53 @@
         load.start()
     for load in loads:
         load.wait()
-    for ex in range(2):
-        for f in range(pieces):
-            hid_local(ex, f).start()
     cot_t[...] = cot_ref[...].T
     routes = routes_ref[...].astype(F32)
-    w0 = weights_ref[...]
-    w1 = w0.astype(BF)
-    rest = w0 - w1.astype(F32)
-    w2 = rest.astype(BF)
-    w3 = (rest - w2.astype(F32)).astype(BF)
-    info = jnp.concatenate(
-        [routes, w1.astype(F32), w2.astype(F32), w3.astype(F32)], axis=0
-    ).astype(BF)
+    info = jnp.concatenate([routes, weights_ref[...]], axis=0).astype(BF)
 
     def columns(section):
         return cot_t[pl.ds(pl.multiple_of(section * width, 16), width), :]
 
     buf_a[0, 0, 0:width, :] = columns(lat_sec)
-    buf_a[0, 0, width : width + 4 * tops, :] = info
+    buf_a[0, 0, width : width + 2 * tops, :] = info
     buf_b[0, 0] = columns(s)
     mir_a[0, 0:width, :] = columns(mirror_s + 1 - 2 * lax.rem(mirror_s, 2))
-    mir_a[0, width : width + 4 * tops, :] = info
+    mir_a[0, width : width + 2 * tops, :] = info
     mir_a[1, 0:width, :] = columns(mirror_s)
     row = lax.broadcasted_iota(jnp.int32, (LANE, LANE), 0)
     col = lax.broadcasted_iota(jnp.int32, (LANE, LANE), 1)
     upper[...] = jnp.where(row < col, 1.0, 0.0).astype(BF)
     pl.semaphore_wait(barrier, 6)
 
-    mir_copies = (
-        remote(mir_a.at[0], buf_a.at[1, 0], mir_s.at[0], mir_r.at[0], mirror),
-        remote(mir_a.at[1, pl.ds(0, width)], buf_b.at[1, 0], mir_s.at[1], mir_r.at[1], mirror),
+    mir_first = [
+        remote(
+            mir_a.at[0, half_of(0, h)],
+            buf_a.at[1, 0, half_of(0, h)],
+            mir_s.at[h],
+            mir_r.at[h],
+            mirror,
+        )
+        for h in range(2)
+    ]
+    mir_second = remote(
+        mir_a.at[1, pl.ds(0, width)], buf_b.at[1, 0], mir_s.at[2], mir_r.at[2], mirror
     )
-    mir_copies[0].start()
     for h in range(2):
+        mir_first[h].start()
         for way in range(2):
             ring(0, way, 0, 1, h).start()
+    for ex in range(2):
+        for f in range(pieces):
+            hid_local(ex, f).start()
 
     experts = [4 * z + 2 * yl, 4 * z + 2 * yl + 1, 4 * z + 2 - 2 * yl, 4 * z + 3 - 2 * yl]
 
     def build(slots):
         masks, gains, combos = [], [], [(sec, slot) for slot in slots for sec in range(2)]
         for sec, slot in combos:
-            data = buf_a[sec, slot, width : width + 4 * tops, :].astype(F32)
+            data = buf_a[sec, slot, width : width + 2 * tops, :].astype(F32)
             named = data[0:tops]
-            gain = data[tops : 2 * tops] + data[2 * tops : 3 * tops] + data[3 * tops : 4 * tops]
+            gain = data[tops : 2 * tops]
             for ex in experts:
                 hit = jnp.where(named == ex.astype(F32), 1.0, 0.0)
                 masks.append(jnp.sum(hit, axis=0, keepdims=True))
@@ -318,11 +324,11 @@
         for ex in range(2):
             turn(1, ex, f, hid_mir)
 
-    mir_copies[0].wait()
     for h in range(2):
+        mir_first[h].wait()
         for way in range(2):
             ring(0, way, 1, 1, h).start()
-    mir_copies[1].start()
+    mir_second.start()
     for f in range(min(DEPTH, pieces)):
         hid_send(f).start()
     build((0,))
@@ -352,7 +358,7 @@
         k = 2 * j + 1
         if ch == 0:
             receive(ch, k, 1 if last else 2)
-            when(j == 1, lambda: mir_copies[1].wait())
+            when(j == 1, lambda: mir_second.wait())
             early(j, 0)
         elif isinstance(j, int):
             if k >= lead:
@@ -450,6 +456,26 @@
         return carry
 
     lax.fori_loop(0, pieces // 2, close_own, 0)
+
+
+def move(parts, src, dst, held, come, go):
+    size = src.shape[2] // parts
+    places = [
+        (p, ex, pl.ds(i * size, size)) for p in range(2) for ex in range(2) for i in range(parts)
+    ]
+    reads = [
+        pltpu.make_async_copy(src.at[at], held.at[at], come.at[i]) for i, at in enumerate(places)
+    ]
+    writes = [
+        pltpu.make_async_copy(held.at[at], dst.at[at], go.at[i]) for i, at in enumerate(places)
+    ]
+    for read in reads:
+        read.start()
+    for read, write in zip(reads, writes):
+        read.wait()
+        write.start()
+    for write in writes:
+        write.wait()
 
 
 def local(routes, weights, cotangent, hidden):
@@ -478,9 +504,9 @@
             pltpu.VMEM((tokens, sections * width), BF),
             dma((3,)),
             pltpu.VMEM((sections * width, tokens), BF),
-            pltpu.VMEM((2, blocks, width + 4 * tops, tokens), BF),
+            pltpu.VMEM((2, blocks, width + 2 * tops, tokens), BF),
             pltpu.VMEM((2, blocks, width, tokens), BF),
-            pltpu.VMEM((2, width + 4 * tops, tokens), BF),
+            pltpu.VMEM((2, width + 2 * tops, tokens), BF),
             pltpu.VMEM((2, pieces, slot_count, LANE), BF),
             pltpu.VMEM((2, pieces, slot_count, LANE), BF),
             pltpu.VMEM((2, 2, units, slot_count), BF),
@@ -495,8 +521,8 @@
             pltpu.VMEM((2, units, width), F32),
             dma((2, 2, 2, half + 1, 2)),
             dma((2, 2, 2, half + 1, 2)),
-            dma((2,)),
-            dma((2,)),
+            dma((3,)),
+            dma((3,)),
             dma((2, pieces)),
             dma((pieces,)),
             dma((pieces,)),
@@ -520,6 +546,14 @@
         cotangent[0],
         hidden[0],
     )
+    grad = pl.pallas_call(
+        functools.partial(move, 2),
+        out_shape=jax.ShapeDtypeStruct(grad.shape, grad.dtype),
+        in_specs=[hbm],
+        out_specs=hbm,
+        scratch_shapes=[pltpu.VMEM(grad.shape, grad.dtype), dma((8,)), dma((8,))],
+        compiler_params=pltpu.CompilerParams(vmem_limit_bytes=63 * 1024 * 1024),
+    )(grad)
     return jnp.swapaxes(grad, 2, 3)
 
 

time: 87.5 us -> 86.3 us (0.986)
  local copies, waits for them, and re-layouts: 2.87 us -> 0 us
  Pallas kernels: 84.2 us -> 85.7 us
    unnamed x1 -> x0, local copies, waits for them, and re-layouts: 2.87 us -> none
    pallas_call x0 -> x1, Pallas kernels: none -> 2.41 us  [local(): pl.pallas_call(functools.partial(move, 2), out_shape=jax.ShapeDtypeStruct...]
    pallas_call x1, Pallas kernels: 84.2 us -> 83.3 us  [local(): pl.pallas_call(functools.partial(kernel, cfg), out_shape=jax.ShapeDtypeSt...]
where the time goes in v3:
time: 86.3 us; the launch traced here: 85.7 us
  Pallas kernels  85.7 us (99%)
    pallas_call x1, Pallas kernels, local(): pl.pallas_call(functools.partial(kernel, cfg), out_shape=jax.ShapeDtypeSt...  83.3 us
    pallas_call x1, Pallas kernels, local(): pl.pallas_call(functools.partial(move, 2), out_shape=jax.ShapeDtypeStruct...  2.41 us

profile of v3, /device:TPU:56, one launch (start us, length us, event | category | flops | bytes accessed | tf_op | source)
XLA Modules:
  0.0 85.7 jit_solution(11531666485101950604)
XLA Ops:
  0.0 83.3 %shard_map.46.src = bf16[2,2,224,1024]{3,2,1,0:T(8,128)(2,1)} custom-call(s32[8,128]{1,0:T(8,128)} %bitcast.11, f32[8,128]{1,0:T(8,128)} %bitcast.12, bf16[128,896]{1,0:T(8,128)(2,1)} %bitcast.10, bf16[2,768,1024]{2,1,0:T(8,128)(2,1)} %bitcast.9), custom_call_target="tpu_custom_call" | custom-call | flops 5637144576 | bytes 8388608 | tf_op jit(solution)/shard_map/pallas_call | solution.py:496
  83.3 2.4 %shard_map.47 = bf16[2,2,224,1024]{3,2,1,0:T(8,128)(2,1)} custom-call(bf16[2,2,224,1024]{3,2,1,0:T(8,128)(2,1)} %shard_map.46.src), custom_call_target="tpu_custom_call" | custom-call | tf_op jit(solution)/shard_map/pallas_call | solution.py:549

commit v4 on v3

--- a/solution.py
+++ b/solution.py
@@ -85,7 +85,7 @@
         )
 
     def half_of(ch, h):
-        total_rows = width + 2 * tops if ch == 0 else width
+        total_rows = width + 4 * tops if ch == 0 else width
         first = (total_rows // 2 + 15) // 16 * 16
         return pl.ds(0, first) if h == 0 else pl.ds(first, total_rows - first)
 
@@ -156,16 +156,23 @@
         load.wait()
     cot_t[...] = cot_ref[...].T
     routes = routes_ref[...].astype(F32)
-    info = jnp.concatenate([routes, weights_ref[...]], axis=0).astype(BF)
+    w0 = weights_ref[...]
+    w1 = w0.astype(BF)
+    rest = w0 - w1.astype(F32)
+    w2 = rest.astype(BF)
+    w3 = (rest - w2.astype(F32)).astype(BF)
+    info = jnp.concatenate(
+        [routes, w1.astype(F32), w2.astype(F32), w3.astype(F32)], axis=0
+    ).astype(BF)
 
     def columns(section):
         return cot_t[pl.ds(pl.multiple_of(section * width, 16), width), :]
 
     buf_a[0, 0, 0:width, :] = columns(lat_sec)
-    buf_a[0, 0, width : width + 2 * tops, :] = info
+    buf_a[0, 0, width : width + 4 * tops, :] = info
     buf_b[0, 0] = columns(s)
     mir_a[0, 0:width, :] = columns(mirror_s + 1 - 2 * lax.rem(mirror_s, 2))
-    mir_a[0, width : width + 2 * tops, :] = info
+    mir_a[0, width : width + 4 * tops, :] = info
     mir_a[1, 0:width, :] = columns(mirror_s)
     row = lax.broadcasted_iota(jnp.int32, (LANE, LANE), 0)
     col = lax.broadcasted_iota(jnp.int32, (LANE, LANE), 1)
@@ -198,9 +205,9 @@
     def build(slots):
         masks, gains, combos = [], [], [(sec, slot) for slot in slots for sec in range(2)]
         for sec, slot in combos:
-            data = buf_a[sec, slot, width : width + 2 * tops, :].astype(F32)
+            data = buf_a[sec, slot, width : width + 4 * tops, :].astype(F32)
             named = data[0:tops]
-            gain = data[tops : 2 * tops]
+            gain = data[tops : 2*tops] + data[2*tops : 3*tops] + data[3*tops : 4*tops]
             for ex in experts:
                 hit = jnp.where(named == ex.astype(F32), 1.0, 0.0)
                 masks.append(jnp.sum(hit, axis=0, keepdims=True))
@@ -504,9 +511,9 @@
             pltpu.VMEM((tokens, sections * width), BF),
             dma((3,)),
             pltpu.VMEM((sections * width, tokens), BF),
-            pltpu.VMEM((2, blocks, width + 2 * tops, tokens), BF),
+            pltpu.VMEM((2, blocks, width + 4 * tops, tokens), BF),
             pltpu.VMEM((2, blocks, width, tokens), BF),
-            pltpu.VMEM((2, width + 2 * tops, tokens), BF),
+            pltpu.VMEM((2, width + 4 * tops, tokens), BF),
             pltpu.VMEM((2, pieces, slot_count, LANE), BF),
             pltpu.VMEM((2, pieces, slot_count, LANE), BF),
             pltpu.VMEM((2, 2, units, slot_count), BF),

time: 86.3 us -> 86.9 us (level)
  no operation moved by 1% of the time
where the time goes in v4:
time: 86.9 us; the launch traced here: 86.3 us
  Pallas kernels  86.3 us (99%)
    pallas_call x1, Pallas kernels, local(): pl.pallas_call(functools.partial(kernel, cfg), out_shape=jax.ShapeDtypeSt...  83.9 us
    pallas_call x1, Pallas kernels, local(): pl.pallas_call(functools.partial(move, 2), out_shape=jax.ShapeDtypeStruct...  2.41 us

profile of v4, /device:TPU:56, one launch (start us, length us, event | category | flops | bytes accessed | tf_op | source)
XLA Modules:
  0.0 86.3 jit_solution(16458464631996834033)
XLA Ops:
  0.0 83.9 %shard_map.46.src = bf16[2,2,224,1024]{3,2,1,0:T(8,128)(2,1)} custom-call(s32[8,128]{1,0:T(8,128)} %bitcast.11, f32[8,128]{1,0:T(8,128)} %bitcast.12, bf16[128,896]{1,0:T(8,128)(2,1)} %bitcast.10, bf16[2,768,1024]{2,1,0:T(8,128)(2,1)} %bitcast.9), custom_call_target="tpu_custom_call" | custom-call | flops 5637144576 | bytes 8388608 | tf_op jit(solution)/shard_map/pallas_call | solution.py:503
  83.9 2.4 %shard_map.47 = bf16[2,2,224,1024]{3,2,1,0:T(8,128)(2,1)} custom-call(bf16[2,2,224,1024]{3,2,1,0:T(8,128)(2,1)} %shard_map.46.src), custom_call_target="tpu_custom_call" | custom-call | tf_op jit(solution)/shard_map/pallas_call | solution.py:556
